TPU v7x, 32 devices: a whole 2x2x4 slice. The times are simulated.
32 devices in a mesh: groups: 2 (over x), attn: 8 (over z, y), ffn: 2 (over core).
Axes of the slice: x: 2, y: 2, z: 4, core: 2. Of those that a mesh axis runs over, the one named last changes fastest.
Arguments:
- queries: bfloat16 [256, 2048], P(('groups', 'attn', 'ffn')), parts along dimension 0, may hold values from -15 to 15
- kv_cache: bfloat16 [2, 262144, 128], P(None, ('groups', 'attn', 'ffn')), parts along dimension 1, may hold values from -4.2 to 4.2
- lengths: int32 [256], P(('groups', 'attn', 'ffn')), parts along dimension 0, may hold values from 1 to 2047, as said below
- hidden: bfloat16 [256, 16384], P('groups', 'attn'), parts along dimension 0, may hold values from -40 to 40
- out_weight: bfloat16 [2048, 16384], P(None, 'attn'), may hold values from -0.125 to 0.125
- norm_gain: bfloat16 [16384], P('attn'), may hold values from 0.099609375 to 1.8984375
- gate_weight: bfloat16 [16384, 3328], P('attn', 'ffn'), may hold values from -0.046875 to 0.046875
- up_weight: bfloat16 [16384, 3328], P('attn', 'ffn'), may hold values from -0.046875 to 0.046875
- down_weight: bfloat16 [3328, 16384], P('ffn', 'attn'), may hold values from -0.109375 to 0.109375
Outputs:
- updated: float32 [256, 16384], P(('groups', 'attn', 'ffn')), parts along dimension 0
There are 2 independent parts, one for each index of `groups`. A program takes and returns all parts, laid end to end along the dimension named above; an argument that names none is the same for every part. Nothing has to cross between parts.
Inputs may be any that keep to these rules, and one draw needn't show every extreme that they name: In each aligned block of 8 requests the lengths sum to at most 8192; some block reaches 8192 and some request reaches 2047 in every draw. Slots after a block's last context hold unused entries.
All inputs are finite; a program needn't handle non-finite values.
Results may differ from a plain program's by a relative error of at most 0.0019.
Values may be sent and summed in bfloat16 or wider, within the bound.
A program may use at most 128 MiB of HBM per device.

v0:
```python
import math

import jax
import jax.numpy as jnp
from jax import lax
from jax.sharding import PartitionSpec as P

D = 16384


big_negative = -1e30
eps = 1e-05


def attend(q_rows, keys, values, starts, ends, last, block):
    count = q_rows.shape[0]
    head_dim = q_rows.shape[1]
    scale = 1.0 / math.sqrt(head_dim)
    turns = (last + block - 1) // block

    def block_scores(index):
        offset = index * block
        key_rows = lax.dynamic_slice_in_dim(keys, offset, block, 0)
        where_tok = offset + jnp.arange(block, dtype=jnp.int32)
        inside = (where_tok[None, :] >= starts[:, None]) & (where_tok[None, :] < ends[:, None])
        scores = (
            lax.dot_general(
                q_rows, key_rows, (((1,), (1,)), ((), ())), preferred_element_type=jnp.float32
            )
            * scale
        )
        return (jnp.where(inside, scores, big_negative), inside, offset)

    def find_peak(index, running):
        scores, inside, offset = block_scores(index)
        return jnp.maximum(running, jnp.max(scores, axis=1))

    peak = lax.fori_loop(0, turns, find_peak, jnp.full((count,), big_negative, jnp.float32))

    def visit(index, carry):
        total, summed = carry
        scores, inside, offset = block_scores(index)
        value_rows = lax.dynamic_slice_in_dim(values, offset, block, 0)
        probs = jnp.where(inside, jnp.exp(scores - peak[:, None]), 0.0)
        total = total + jnp.sum(probs, axis=1)
        summed = summed + jnp.dot(
            probs.astype(jnp.bfloat16), value_rows, preferred_element_type=jnp.float32
        )
        return (total, summed)

    init = (jnp.zeros((count,), jnp.float32), jnp.zeros((count, head_dim), jnp.float32))
    total, summed = lax.fori_loop(0, turns, visit, init)
    return (peak, total, summed)


def per_device(
    queries, kv_cache, lengths, hidden, out_weight, norm_gain, gate_weight, up_weight, down_weight
):
    req_dev, width = queries.shape
    head_dim = kv_cache.shape[2]
    slots = kv_cache.shape[1]
    heads = width // head_dim
    block = min(512, slots // 2)
    n_attn = lax.axis_size("attn")
    n_ffn = lax.axis_size("ffn")
    ends = jnp.cumsum(lengths)
    starts = ends - lengths
    used = ends[-1]
    q_rows = queries.reshape(req_dev * heads, head_dim)
    row_starts = jnp.repeat(starts, heads)
    row_ends = jnp.repeat(ends, heads)
    peak, total, summed = attend(
        q_rows, kv_cache[0], kv_cache[1], row_starts, row_ends, used, block
    )
    attended = (summed / total[:, None]).astype(jnp.bfloat16).reshape(req_dev, width)
    heads_part = jnp.dot(
        lax.all_gather(attended, ("attn", "ffn"), axis=0, tiled=True),
        out_weight,
        preferred_element_type=jnp.float32,
    )
    mixed = hidden.astype(jnp.float32) + heads_part
    squares = lax.psum(jnp.sum(mixed * mixed, axis=1), "attn")
    inverse = lax.rsqrt(squares / D + eps)
    normed = (mixed * inverse[:, None] * norm_gain.astype(jnp.float32)).astype(jnp.bfloat16)
    gate_part = jnp.dot(normed, gate_weight, preferred_element_type=jnp.float32)
    up_part = jnp.dot(normed, up_weight, preferred_element_type=jnp.float32)
    gate, up = lax.psum((gate_part, up_part), "attn")
    units = (jax.nn.silu(gate) * up).astype(jnp.bfloat16)
    down = jnp.dot(units, down_weight, preferred_element_type=jnp.float32)
    cols = down.shape[1]
    grid_down = down.reshape(n_attn, n_ffn, req_dev, cols)
    summed_down = lax.psum_scatter(grid_down, "ffn", scatter_dimension=1, tiled=True)
    own_index = lax.axis_index("ffn")
    own_mixed = lax.dynamic_slice_in_dim(
        mixed.reshape(n_attn, n_ffn, req_dev, cols), own_index, 1, 1
    )
    finished = summed_down + own_mixed
    gathered_rows = lax.all_to_all(finished, "attn", split_axis=0, concat_axis=3, tiled=True)
    return gathered_rows.reshape(req_dev, cols * n_attn)


def solution(mesh):
    return jax.shard_map(
        per_device,
        mesh=mesh,
        in_specs=(
            P(("groups", "attn", "ffn"), None),
            P(None, ("groups", "attn", "ffn"), None),
            P(("groups", "attn", "ffn")),
            P("groups", "attn"),
            P(None, "attn"),
            P("attn"),
            P("attn", "ffn"),
            P("attn", "ffn"),
            P("ffn", "attn"),
        ),
        out_specs=P(("groups", "attn", "ffn"), None),
        check_vma=False,
    )
```

profile of v0, /device:TPU:0, one launch (start us, length us, event | category | flops | bytes accessed | tf_op | source)
XLA Modules:
  0.0 268.4 jit_solution(9166724689828984766)
XLA Ops:
  9.4 3.8 %slice_bitcast_fusion = (bf16[8192,128]{1,0:T(8,128)(2,1)S(1)}, bf16[8192,128]{1,0:T(8,128)(2,1)}) fusion(bf16[2,8192,128]{2,1,0:T(8,128)(2,1)} %param.14), kind=kLoop, calls=%fused_computation.25 | loop fusion | bytes 8388608 | tf_op jit(solution)/shard_map/squeeze | solution.py:73
  13.3 23.9 %while.24 = (s32[]{:T(128)}, f32[128]{0:T(128)S(1)}, s32[]{:T(128)}, bf16[8192,128]{1,0:T(8,128)(2,1)}, bf16[128,128]{1,0:T(8,128)(2,1)S(1)}, /*index=5*/s32[8]{...) while((s32[]{:T(128)}, f32[128]{0:T(128)S(1)}, s32[]{:T(128)}, ...), condition=%wide.region_3.4_spmd.clone, body=%wide.region_1.3_spmd.clone.sunk | while | flops 17170948 | bytes 174315 | solution.py:38
  19.6 1.2 fusion.46
  25.6 1.2 fusion.46
  30.0 1.2 fusion.46
  37.2 28.1 %while.25 = (s32[]{:T(128)}, f32[128]{0:T(128)S(1)}, f32[128,128]{1,0:T(8,128)S(1)}, s32[]{:T(128)}, bf16[8192,128]{1,0:T(8,128)(2,1)}, /*index=5*/bf16[128,128]...) while((s32[]{:T(128)}, f32[128]{0:T(128)S(1)}, ...), condition=%wide.region_6.7_spmd.clone, body=%wide.region_4.6_spmd.clone.sunk | while | flops 34161156 | bytes 699143 | solution.py:52
  37.5 1.2 fusion.50
  39.3 1.2 fusion.50
  41.0 1.2 fusion.50
  42.8 1.2 fusion.50
  44.6 1.2 fusion.50
  46.3 1.2 fusion.50
  48.1 1.2 fusion.50
  49.8 1.2 fusion.50
  51.6 1.2 fusion.50
  53.3 1.2 fusion.50
  55.1 1.2 fusion.50
  56.9 1.2 fusion.50
  58.6 1.2 fusion.50
  60.4 1.2 fusion.50
  62.1 1.2 fusion.50
  63.9 1.2 fusion.50
  65.5 20.2 %all_gather.3 = bf16[128,2048]{1,0:T(8,128)(2,1)S(1)} all-gather(bf16[8,2048]{1,0:T(8,128)(2,1)S(1)} %reshape.45), channel_id=1, replica_groups=mesh['groups'=2,'attn'=8,'ffn'=2] {'attn','ffn'}, dimensions={0}, use_global_device_ids=true | all-gather | bytes 557056 | tf_op jit(solution)/shard_map/all_gather | solution.py:77
  85.6 4.8 %multiply_reduce_fusion = (f32[128]{0:T(128)S(1)}, f32[128,2048]{1,0:T(8,128)S(1)}) fusion(bf16[128,2048]{1,0:T(8,128)(2,1)S(1)} %all_gather.3, bf16[2048,2048]{1,0:T(8,128)(2,1)} %param.17, bf16[128,2048]{1,0:T(8,128)(2,1)S(1)} %copy-done), kind=kOutput, calls=%fused_computation.28 | convolution fusion | flops 1074790272 | bytes 10486272 | tf_op jit(solution)/shard_map/dot_general | solution.py:76
  90.4 17.7 %psum.21 = f32[128]{0:T(128)S(1)} all-reduce(f32[128]{0:T(128)S(1)} %get-tuple-element.186), channel_id=1, replica_groups=mesh['groups'=2,'attn'=8,'ffn'=2] {'attn'}, use_global_device_ids=true, to_apply=%region_8.9 | all-reduce | flops 128 | bytes 1024 | tf_op jit(solution)/shard_map/psum | solution.py:82
  108.1 5.0 %fusion.26 = f32[128,1664]{1,0:T(8,128)} fusion(bf16[2048,1664]{1,0:T(8,128)(2,1)} %param.20, f32[128,2048]{1,0:T(8,128)S(1)} %get-tuple-element.187, f32[2048]{0:T(1024)S(1)} %convert_element_type.20, f32[128]{0:T(128)S(1)} %add_rsqrt_fusion), kind=kOutput, calls=%fused_computation.37 | convolution fusion | flops 873201664 | bytes 8724992 | tf_op jit(solution)/shard_map/dot_general | solution.py:86
  113.1 5.0 %fusion.27 = f32[128,1664]{1,0:T(8,128)} fusion(bf16[2048,1664]{1,0:T(8,128)(2,1)} %param.19, f32[128,2048]{1,0:T(8,128)S(1)} %get-tuple-element.187, f32[2048]{0:T(1024)S(1)} %convert_element_type.20, f32[128]{0:T(128)S(1)} %add_rsqrt_fusion), kind=kOutput, calls=%fused_computation.38 | convolution fusion | flops 873201664 | bytes 8724992 | tf_op jit(solution)/shard_map/dot_general | solution.py:85
  118.2 95.5 %all-reduce.7.cloned.1.call-done = (f32[128,1664]{1,0:T(8,128)}, f32[128,1664]{1,0:T(8,128)}) async-done(((f32[128,1664]{1,0:T(8,128)}, f32[128,1664]{1,0:T(8,128)}), (f32[128,1664]{1,0:T(8,128)}, f32[128,1664]{1,0:T(8,128)})) %all-reduce.7.cloned.1.call-update) | async-done | bytes 1703952 | tf_op jit(solution)/shard_map/psum | solution.py:87
  213.6 5.6 %fusion.23 = f32[128,2048]{1,0:T(8,128)} fusion(bf16[1664,2048]{1,0:T(8,128)(2,1)} %param.21, f32[128,1664]{1,0:T(8,128)} %get-tuple-element.180, f32[128,1664]{1,0:T(8,128)} %get-tuple-element.181), kind=kOutput, calls=%fused_computation.31 | convolution fusion | flops 873693184 | bytes 9568256 | tf_op jit(solution)/shard_map/dot_general | solution.py:89
  219.9 18.6 %all-reduce.5.cloned.1.call-done = f32[8,2,8,2048]{3,2,1,0:T(8,128)} async-done(((f32[8,2,8,2048]{3,2,1,0:T(8,128)}), f32[8,2,8,2048]{3,2,1,0:T(8,128)}) %all-reduce.5.cloned.1.call-update) | async-done | bytes 1048592
  238.5 1.7 dynamic-slice_add_fusion
  240.3 20.5 %all_to_all.15 = f32[8,1,8,2048]{3,2,1,0:T(8,128)S(1)} all-to-all(f32[8,1,8,2048]{3,2,1,0:T(8,128)S(1)} %dynamic-slice_add_fusion), channel_id=1, replica_groups=mesh['groups'=2,'attn'=8,'ffn'=2] {'attn'}, dimensions={0} | all-to-all | bytes 1048576 | tf_op jit(solution)/shard_map/all_to_all | solution.py:98
  (246 shorter events, 32.6 us)
Async XLA Ops:
  6.5 6.7 %copy-start.1 = (bf16[8,2048]{1,0:T(8,128)(2,1)S(1)}, bf16[8,2048]{1,0:T(8,128)(2,1)}, u32[]{:S(2)}) copy-start(bf16[8,2048]{1,0:T(8,128)(2,1)} %param.13) | copy-start | bytes 98308
  6.5 207.1 %all-reduce.7.cloned.1.call-start = ((), (), s32[]{:S(2)}) async-start(), calls=%async_computation.2 | async-start | bytes 3407872 | tf_op jit(solution)/shard_map/psum | solution.py:87
  13.3 72.4 %copy-start.2 = (bf16[2048]{0:T(1024)(128)(2,1)S(1)}, bf16[2048]{0:T(1024)(128)(2,1)}, u32[]{:S(2)}) copy-start(bf16[2048]{0:T(1024)(128)(2,1)} %param.18) | copy-start | bytes 12292
  13.3 72.4 %copy-start = (bf16[128,2048]{1,0:T(8,128)(2,1)S(1)}, bf16[128,2048]{1,0:T(8,128)(2,1)}, u32[]{:S(2)}) copy-start(bf16[128,2048]{1,0:T(8,128)(2,1)} %param.16) | copy-start | bytes 1572868
  118.1 101.2 %copy-start.3 = (u32[32]{0:T(128)S(1)}, u32[32]{0:T(128)}, u32[]{:S(2)}) copy-start(u32[32]{0:T(128)} %constant.77) | copy-start | bytes 388
  118.1 120.4 %all-reduce.5.cloned.1.call-start = ((), (), s32[]{:S(2)}) async-start(), calls=%async_computation.1 | async-start | bytes 2097152
Sparse Core Ops, SparseCore 0:
  118.3 95.3 all-reduce.6
  219.4 19.0 all-reduce.4
where the time goes:
time: 268 us
  waiting for transfers between devices  114 us (43%)
  matrix products  61.4 us (23%)
  blocking collectives  58.3 us (22%)
  local copies, waits for them, and re-layouts  15.6 us (6%)
  between operations  14.2 us (5%)
  other arithmetic  3.84 us (1%)
    psum x1, waiting for transfers between devices, per_device(): gate, up = lax.psum((gate_part, up_part), 'attn')  95.5 us
    dot_general x32, matrix products, block_scores(): lax.dot_general(q_rows, key_rows, (((1,), (1,)), ((), ())), preferred_ele...  37.2 us
    all_to_all x1, blocking collectives, per_device(): lax.all_to_all(finished, 'attn', split_axis=0, concat_axis=3, tiled=True)  20.5 us
    all_gather x1, blocking collectives, per_device(): lax.all_gather(attended, ('attn', 'ffn'), axis=0, tiled=True)  20.2 us
    unnamed x3, waiting for transfers between devices  18.7 us
    psum x1, blocking collectives, per_device(): squares = lax.psum(jnp.sum(mixed * mixed, axis=1), 'attn')  17.7 us
    dot_general x1, matrix products, per_device(): down = jnp.dot(units, down_weight, preferred_element_type=jnp.float32)  5.61 us
  transfers between devices with their start and end apart: 2, of which 2 were waited for; matrix products, arithmetic and copies ran while one was open for 0% of the time, Pallas kernels for 0%

commit v1 on v0

v1 whole, which is shorter than its diff:
```python
import functools
import math

import jax
import jax.numpy as jnp
from jax import lax
from jax.experimental import pallas as pl
from jax.experimental.pallas import tpu as pltpu
from jax.sharding import PartitionSpec as P

F32 = jnp.float32
BF16 = jnp.bfloat16
EPS = 1e-05
NEG = -1e30
TILES = 2


def unit_chunks(units):
    tiles = units // 128
    marks = [0, (tiles * 3) // 13, (tiles * 7) // 13, (tiles * 11) // 13, tiles]
    return [(lo * 128, (hi - lo) * 128) for lo, hi in zip(marks, marks[1:])]


def fold(x):
    half = x.shape[1] // 2
    return jnp.concatenate([x[:, :half], x[:, half:]], axis=0)


def unfold(x):
    rows = x.shape[0] // 2
    return jnp.concatenate([x[:rows], x[rows:]], axis=1)


def kernel(n, names, *refs):
    (q_ref, kv_ref, len_ref, hid_ref, wo_ref, gain_ref, wg_ref, wu_ref, wd_ref, out_ref) = refs[:10]
    s = dict(zip(names, refs[10:]))
    a = lax.axis_index("attn")
    f = lax.axis_index("ffn")
    nh = n // 2
    me = a * 2 + f
    pa = lax.rem(a, 2)
    ja = a // 2
    partner = {"attn": a + 1 - 2 * pa, "ffn": f}
    sibling = {"attn": a, "ffn": 1 - f}
    req, width = q_ref.shape
    slots, hd = s["k"].shape
    heads = width // hd
    rows = n * 16
    cols = hid_ref.shape[1]
    units = wg_ref.shape[1]
    cuts = unit_chunks(units)
    tw = cols // TILES

    def remote(src, dst, ssem, rsem, dev):
        return pltpu.make_async_remote_copy(
            src_ref=src, dst_ref=dst, send_sem=ssem, recv_sem=rsem,
            device_id=dev, device_id_type=pl.DeviceIdType.MESH)

    def local(src, dst, i):
        return pltpu.make_async_copy(src, dst, s["loc"].at[i])

    cp_k = local(kv_ref.at[0], s["k"], 0)
    cp_v = local(kv_ref.at[1], s["v"], 1)
    cp_h = local(hid_ref, s["hid"], 2)
    cp_o = local(wo_ref, s["wo"], 3)
    cp_g = local(wg_ref, s["wg"], 4)
    cp_u = local(wu_ref, s["wu"], 5)
    cp_d = local(wd_ref, s["wd"], 6)
    cp_h.start()
    cp_k.start()
    cp_v.start()

    barrier = pltpu.get_barrier_semaphore()

    @pl.loop(1, 2 * n)
    def _(i):
        d = lax.rem(me + i, 2 * n)
        pl.semaphore_signal(barrier, inc=1, device_id={"attn": d // 2, "ffn": lax.rem(d, 2)},
                            device_id_type=pl.DeviceIdType.MESH)

    cp_h.wait()
    pl.semaphore_wait(barrier, 2 * n - 1)

    def own_rows(b):
        blk = s["hid"][pl.ds(pl.multiple_of(b * 16, 16), 16), :].astype(F32)
        return jnp.where(f == 0, blk[:8], blk[8:])

    def hid_copy(b):
        return remote(s["hid_send"].at[b], s["hid_recv"].at[a], s["hid_s"].at[b], s["hid_r"].at[a],
                      {"attn": b, "ffn": f})

    x = own_rows(a)
    for t in range(TILES):
        s["hid_recv"][a, t] = fold(x[:, t * tw:(t + 1) * tw]).astype(BF16)

    @pl.loop(1, n)
    def _(i):
        b = lax.rem(a + i, n)
        x = own_rows(b)
        for t in range(TILES):
            s["hid_send"][b, t] = fold(x[:, t * tw:(t + 1) * tw]).astype(BF16)
        hid_copy(b).start()

    q32 = q_ref[...].astype(F32)
    qs = jnp.concatenate([q32[:, g * hd:(g + 1) * hd] for g in range(heads)], axis=0).astype(BF16)
    at_row = lax.broadcasted_iota(jnp.int32, (req, 1), 0)
    starts = jnp.zeros((req, 1), jnp.int32)
    ends = jnp.zeros((req, 1), jnp.int32)
    run = jnp.int32(0)
    for i in range(req):
        starts = jnp.where(at_row == i, run, starts)
        run = run + len_ref[i]
        ends = jnp.where(at_row == i, run, ends)
    tc = min(1024, slots)
    qr = req * heads
    cp_k.wait()
    cp_o.start()

    def first(k, m):
        off = pl.multiple_of(k * tc, tc)
        sc = lax.dot_general(qs, s["k"][pl.ds(off, tc), :], (((1,), (1,)), ((), ())),
                             preferred_element_type=F32)
        slot = off + lax.broadcasted_iota(jnp.int32, (req, tc), 1)
        inside = (slot >= starts) & (slot < ends)
        sc = jnp.where(inside[None], sc.reshape(heads, req, tc), NEG).reshape(qr, tc)
        s["sc"][:, pl.ds(off, tc)] = sc
        for t in range(tc // 128):
            m = jnp.maximum(m, sc[:, t * 128:(t + 1) * 128])
        return m

    m = lax.fori_loop(0, slots // tc, first, jnp.full((qr, 128), NEG, F32))
    peak = jnp.max(m, axis=1, keepdims=True)
    cp_v.wait()
    cp_g.start()
    cp_u.start()
    cp_d.start()

    scale2 = 1.4426950408889634 / math.sqrt(hd)

    def second(k, carry):
        tot, acc = carry
        off = pl.multiple_of(k * tc, tc)
        p = jnp.exp2((s["sc"][:, pl.ds(off, tc)] - peak) * scale2)
        for t in range(tc // 128):
            tot = tot + p[:, t * 128:(t + 1) * 128]
        acc = acc + jnp.dot(p.astype(BF16), s["v"][pl.ds(off, tc), :], preferred_element_type=F32)
        return tot, acc

    tot, acc = lax.fori_loop(0, slots // tc, second,
                             (jnp.zeros((qr, 128), F32), jnp.zeros((qr, hd), F32)))
    att = acc / jnp.sum(tot, axis=1, keepdims=True)
    att = jnp.concatenate([att[g * req:(g + 1) * req] for g in range(heads)], axis=1)
    s["att"][ja, pa, f] = fold(att).astype(BF16)

    def aa_copy(j):
        blk = s["att"].at[ja, pa, f]
        return remote(blk, blk, s["aa_s"].at[j], s["aa_r"].at[ja], {"attn": 2 * j + pa, "ffn": f})

    def ab_copy(j):
        blk = s["att"].at[j, pa, f]
        return remote(blk, blk, s["ab_s"].at[j], s["ab_r"].at[j], partner)

    def ac_copy(j, par):
        blk = s["att"].at[j, par, f]
        return remote(blk, blk, s["ac_s"].at[j, par], s["ac_r"].at[j, par], sibling)

    @pl.loop(1, nh)
    def _(i):
        aa_copy(lax.rem(ja + i, nh)).start()

    ab_copy(ja).start()
    ac_copy(ja, pa).start()

    @pl.loop(1, nh)
    def _(i):
        j = lax.rem(ja + i, nh)
        blk = s["att"].at[j, pa, f]
        remote(blk, blk, s["aa_s"].at[j], s["aa_r"].at[j], {"attn": 2 * j + pa, "ffn": f}).wait_recv()
        ab_copy(j).start()
        ac_copy(j, pa).start()

    @pl.loop(0, nh)
    def _(i):
        j = lax.rem(ja + i, nh)
        blk = s["att"].at[j, 1 - pa, f]
        remote(blk, blk, s["ab_s"].at[j], s["ab_r"].at[j], partner).wait_recv()
        ac_copy(j, 1 - pa).start()

    @pl.loop(0, nh)
    def _(i):
        j = lax.rem(ja + i, nh)
        for k in range(2):
            par = pa if k == 0 else 1 - pa
            blk = s["att"].at[j, par, 1 - f]
            remote(blk, blk, s["ac_s"].at[j, par], s["ac_r"].at[j, par], sibling).wait_recv()

    @pl.loop(0, n)
    def _(p):
        pair = [unfold(s["att"][p // 2, lax.rem(p, 2), k].astype(F32)) for k in range(2)]
        s["heads_in"][pl.ds(pl.multiple_of(p * 16, 16), 16), :] = jnp.concatenate(pair, axis=0).astype(BF16)

    cp_o.wait()
    mt = min(512, cols)

    def project(t, sq):
        c = pl.ds(pl.multiple_of(t * mt, mt), mt)
        hp = jnp.dot(s["heads_in"][...], s["wo"][:, c], preferred_element_type=F32)
        s["heads"][:, c] = hp
        mx = hp + s["hid"][:, c].astype(F32)
        s["h"][:, c] = (mx * gain_ref[c].astype(F32).reshape(1, mt)).astype(BF16)
        for k in range(mt // 128):
            y = mx[:, k * 128:(k + 1) * 128]
            sq = sq + y * y
        return sq

    sq = lax.fori_loop(0, cols // mt, project, jnp.zeros((rows, 128), F32))
    sq = jnp.broadcast_to(jnp.sum(sq, axis=1, keepdims=True), (rows, 128))
    s["sq_recv"][a] = jnp.transpose(sq)[:8]

    def sq_copy(b):
        return remote(s["sq_recv"].at[a], s["sq_recv"].at[a], s["sq_s"].at[b], s["sq_r"].at[a],
                      {"attn": b, "ffn": f})

    @pl.loop(1, n)
    def _(i):
        sq_copy(lax.rem(a + i, n)).start()

    def s1_copy(c):
        return remote(s["s1_send%d" % c], s["s1_recv%d" % c], s["s1_s"].at[c], s["s1_r"].at[c], partner)

    def s2_copy(c, j):
        return remote(s["s2_send%d" % c].at[j], s["s2_recv%d" % c].at[ja], s["s2_s"].at[c, j], s["s2_r"].at[c, ja],
                      {"attn": 2 * j + pa, "ffn": f})

    def ua_copy(c, j):
        blk = s["u%d" % c].at[ja, pa]
        return remote(blk, blk, s["ua_s"].at[c, j], s["ua_r"].at[c, ja], {"attn": 2 * j + pa, "ffn": f})

    def ub_copy(c, j):
        blk = s["u%d" % c].at[j, pa]
        return remote(blk, blk, s["ub_s"].at[c, j], s["ub_r"].at[c, j], partner)

    def gate_up(c):
        at, w = cuts[c]
        part = s["part%d" % c]
        for k, wt in enumerate(("wg", "wu")):
            r = jnp.dot(s["h"][...], s[wt][:, at:at + w], preferred_element_type=F32)
            part[:, :, :, k * w:(k + 1) * w] = r.reshape(nh, 2, 16, w)

        @pl.loop(0, nh)
        def _(j):
            s["s1_send%d" % c][j] = part[j, 1 - pa].astype(BF16)

        s1_copy(c).start()

    def pair_sum(c):
        s1_copy(c).wait_recv()
        part = s["part%d" % c]

        @pl.loop(1, nh)
        def _(i):
            j = lax.rem(ja + i, nh)
            s["s2_send%d" % c][j] = (part[j, pa] + s["s1_recv%d" % c][j].astype(F32)).astype(BF16)
            s2_copy(c, j).start()

    def make_units(c, inv):
        at, w = cuts[c]
        total = s["part%d" % c][ja, pa] + s["s1_recv%d" % c][ja].astype(F32)

        def body(i, total):
            j = lax.rem(ja + i, nh)
            blk = s["s2_recv%d" % c].at[j]
            remote(blk, blk, s["s2_s"].at[c, j], s["s2_r"].at[c, j], {"attn": 2 * j + pa, "ffn": f}).wait_recv()
            return total + blk[...].astype(F32)

        total = lax.fori_loop(1, nh, body, total)
        gate = total[:, :w] * inv
        up = total[:, w:] * inv
        s["u%d" % c][ja, pa] = (gate / (1.0 + jnp.exp(-gate)) * up).astype(BF16)

        @pl.loop(1, nh)
        def _(i):
            ua_copy(c, lax.rem(ja + i, nh)).start()

        ub_copy(c, ja).start()

    def forward(c):
        @pl.loop(1, nh)
        def _(i):
            j = lax.rem(ja + i, nh)
            blk = s["u%d" % c].at[j, pa]
            remote(blk, blk, s["ua_s"].at[c, j], s["ua_r"].at[c, j], {"attn": 2 * j + pa, "ffn": f}).wait_recv()
            ub_copy(c, j).start()

    def take_units(c):
        @pl.loop(0, nh)
        def _(j):
            blk = s["u%d" % c].at[j, 1 - pa]
            remote(blk, blk, s["ub_s"].at[c, j], s["ub_r"].at[c, j], partner).wait_recv()

    def down(c, t):
        at, w = cuts[c]
        mtd = min(512, tw)
        u = s["u%d" % c][...].reshape(rows, w)

        @pl.loop(0, tw // mtd)
        def _(k):
            col = pl.ds(pl.multiple_of(t * tw + k * mtd, mtd), mtd)
            loc = pl.ds(pl.multiple_of(k * mtd, mtd), mtd)
            r = jnp.dot(u, s["wd"][at:at + w, col], preferred_element_type=F32).reshape(n, 2, 8, mtd)
            if c > 0:
                r = r + s["down"][t, :, :, :, loc]
            s["down"][t, :, :, :, loc] = r

    cp_g.wait()
    cp_u.wait()
    gate_up(0)

    @pl.loop(1, n)
    def _(i):
        b = lax.rem(a + i, n)
        blk = s["sq_recv"].at[b]
        remote(blk, blk, s["sq_s"].at[b], s["sq_r"].at[b], {"attn": b, "ffn": f}).wait_recv()

    inv = lax.rsqrt(jnp.sum(s["sq_recv"][...], axis=0)[:1] / (n * cols) + EPS)
    s["inv"][...] = jnp.transpose(jnp.broadcast_to(inv, (128, rows)))

    @pl.loop(0, cols // mt)
    def _(t):
        c = pl.ds(pl.multiple_of(t * mt, mt), mt)
        mx = s["heads"][:, c] + s["hid"][:, c].astype(F32)
        s["h"][:, c] = (mx * s["inv"][:, :1] * gain_ref[c].astype(F32).reshape(1, mt)).astype(BF16)

    own_inv = s["inv"][pl.ds(pl.multiple_of(a * 16, 16), 16), :1]
    gate_up(1)
    pair_sum(0)
    gate_up(2)
    pair_sum(1)
    gate_up(3)
    make_units(0, own_inv)
    pair_sum(2)
    make_units(1, 1.0)
    forward(0)
    pair_sum(3)
    make_units(2, 1.0)
    forward(1)
    cp_d.wait()
    take_units(0)
    for t in range(TILES):
        down(0, t)
    make_units(3, 1.0)
    forward(2)
    take_units(1)
    for t in range(TILES):
        down(1, t)
    forward(3)
    take_units(2)
    for t in range(TILES):
        down(2, t)
    take_units(3)

    def sib_copy(t):
        return remote(s["down"].at[t, :, 1 - f], s["sib_recv"].at[t], s["sib_s"].at[t], s["sib_r"].at[t], sibling)

    def fin_copy(t, b):
        return remote(s["fin_send"].at[t, b], s["fin_recv"].at[t, a], s["fin_s"].at[t, b], s["fin_r"].at[t, a],
                      {"attn": b, "ffn": f})

    for t in range(TILES):
        down(3, t)
        sib_copy(t).start()
    for t in range(TILES):
        sib_copy(t).wait_recv()

        def added(b):
            hp = s["heads"][pl.ds(pl.multiple_of(b * 16, 16), 16), t * tw:(t + 1) * tw]
            hp = jnp.where(f == 0, hp[:8], hp[8:])
            return fold(s["down"][t, b, f] + s["sib_recv"][t, b] + hp)

        @pl.loop(1, n)
        def _(i):
            b = lax.rem(a + i, n)
            s["fin_send"][t, b] = added(b).astype(BF16)
            fin_copy(t, b).start()

        s["fin_recv"][t, a] = added(a).astype(BF16)

    def put(b):
        for t in range(TILES):
            y = unfold(s["hid_recv"][b, t].astype(F32) + s["fin_recv"][t, b].astype(F32))
            out_ref[:, pl.ds(pl.multiple_of(b * cols + t * tw, tw), tw)] = y

    put(a)

    @pl.loop(1, n)
    def _(i):
        b = lax.rem(a + i, n)
        blk = s["hid_recv"].at[b]
        remote(blk, blk, s["hid_s"].at[b], s["hid_r"].at[b], {"attn": b, "ffn": f}).wait_recv()
        for t in range(TILES):
            blk = s["fin_recv"].at[t, b]
            remote(blk, blk, s["fin_s"].at[t, b], s["fin_r"].at[t, b], {"attn": b, "ffn": f}).wait_recv()
        put(b)

    @pl.loop(1, nh)
    def _(i):
        aa_copy(lax.rem(ja + i, nh)).wait_send()

    @pl.loop(0, nh)
    def _(j):
        ab_copy(j).wait_send()
        for par in range(2):
            ac_copy(j, par).wait_send()

    @pl.loop(1, n)
    def _(i):
        b = lax.rem(a + i, n)
        hid_copy(b).wait_send()
        sq_copy(b).wait_send()
        for t in range(TILES):
            fin_copy(t, b).wait_send()

    for c in range(len(cuts)):
        s1_copy(c).wait_send()
        ub_copy(c, ja).wait_send()

        @pl.loop(1, nh)
        def _(i):
            j = lax.rem(ja + i, nh)
            s2_copy(c, j).wait_send()
            ua_copy(c, j).wait_send()
            ub_copy(c, j).wait_send()

    for t in range(TILES):
        sib_copy(t).wait_send()


def per_device(n, queries, kv_cache, lengths, hidden, out_weight, norm_gain, gate_weight, up_weight, down_weight):
    req, width = queries.shape
    slots, hd = kv_cache.shape[1:]
    rows, cols = hidden.shape
    units = gate_weight.shape[1]
    nh = n // 2
    tw = cols // TILES
    cuts = unit_chunks(units)
    nc = len(cuts)
    V, D = pltpu.VMEM, pltpu.SemaphoreType.DMA
    sc = {
        "k": V((slots, hd), BF16), "v": V((slots, hd), BF16), "hid": V((rows, cols), BF16),
        "wo": V(out_weight.shape, BF16), "wg": V(gate_weight.shape, BF16), "wu": V(up_weight.shape, BF16),
        "wd": V(down_weight.shape, BF16), "sc": V((req * width // hd, slots), F32),
        "hid_send": V((n, TILES, 16, tw // 2), BF16), "hid_recv": V((n, TILES, 16, tw // 2), BF16),
        "att": V((nh, 2, 2, 16, width // 2), BF16), "heads_in": V((rows, width), BF16),
        "heads": V((rows, cols), F32), "h": V((rows, cols), BF16),
        "sq_recv": V((n, 8, rows), F32), "inv": V((rows, 128), F32),
        "down": V((TILES, n, 2, 8, tw), F32), "sib_recv": V((TILES, n, 8, tw), F32),
        "fin_send": V((TILES, n, 16, tw // 2), BF16), "fin_recv": V((TILES, n, 16, tw // 2), BF16),
        "loc": D((7,)), "aa_s": D((nh,)), "aa_r": D((nh,)), "ab_s": D((nh,)), "ab_r": D((nh,)),
        "ac_s": D((nh, 2)), "ac_r": D((nh, 2)), "hid_s": D((n,)), "hid_r": D((n,)),
        "sq_s": D((n,)), "sq_r": D((n,)), "s1_s": D((nc,)), "s1_r": D((nc,)),
        "s2_s": D((nc, nh)), "s2_r": D((nc, nh)), "ua_s": D((nc, nh)), "ua_r": D((nc, nh)),
        "ub_s": D((nc, nh)), "ub_r": D((nc, nh)), "sib_s": D((TILES,)), "sib_r": D((TILES,)),
        "fin_s": D((TILES, n)), "fin_r": D((TILES, n)),
    }
    for c, (_, w) in enumerate(cuts):
        sc["part%d" % c] = V((nh, 2, 16, 2 * w), F32)
        for name in ("s1_send", "s1_recv", "s2_send", "s2_recv"):
            sc["%s%d" % (name, c)] = V((nh, 16, 2 * w), BF16)
        sc["u%d" % c] = V((nh, 2, 16, w), BF16)
    hbm = pl.BlockSpec(memory_space=pl.ANY)
    vmem = pl.BlockSpec(memory_space=pltpu.VMEM)
    smem = pl.BlockSpec(memory_space=pltpu.SMEM)
    return pl.pallas_call(
        functools.partial(kernel, n, tuple(sc)),
        out_shape=jax.ShapeDtypeStruct((req, cols * n), F32),
        in_specs=[vmem, hbm, smem, hbm, hbm, vmem, hbm, hbm, hbm],
        out_specs=vmem,
        scratch_shapes=list(sc.values()),
        compiler_params=pltpu.CompilerParams(collective_id=0, has_side_effects=True,
                                             vmem_limit_bytes=58 * 1024 * 1024),
    )(queries, kv_cache, lengths, hidden, out_weight, norm_gain, gate_weight, up_weight, down_weight)


def solution(mesh):
    return jax.shard_map(
        functools.partial(per_device, mesh.shape["attn"]),
        mesh=mesh,
        in_specs=(
            P(("groups", "attn", "ffn"), None),
            P(None, ("groups", "attn", "ffn"), None),
            P(("groups", "attn", "ffn")),
            P("groups", "attn"),
            P(None, "attn"),
            P("attn"),
            P("attn", "ffn"),
            P("attn", "ffn"),
            P("ffn", "attn"),
        ),
        out_specs=P(("groups", "attn", "ffn"), None),
        check_vma=False,
    )
```

time: 268 us -> 64.5 us (0.24)
  waiting for transfers between devices: 114 us -> 0 us
  Pallas kernels: 0 us -> 62.4 us
  matrix products: 61.4 us -> 0 us
  blocking collectives: 58.3 us -> 0 us
  between operations: 14.2 us -> 0.01 us
  local copies, waits for them, and re-layouts: 15.6 us -> 1.87 us
  other arithmetic: 3.84 us -> 0 us
    psum x1 -> x0, waiting for transfers between devices: 95.5 us -> none  [per_device(): gate, up = lax.psum((gate_part, up_part), 'attn')]
    pallas_call x0 -> x1, Pallas kernels: none -> 62.4 us  [per_device(): pl.pallas_call(functools.partial(kernel, n, tuple(sc)), out_shape=jax.Sha...]
    dot_general x52 -> x0, matrix products: 61.4 us -> none  [the longest x32 37.2 us: block_scores(): lax.dot_general(q_rows, key_rows, (((1,), (1,)), ((), ())), preferred_ele...]
    all_to_all x1 -> x0, blocking collectives: 20.5 us -> none  [per_device(): lax.all_to_all(finished, 'attn', split_axis=0, concat_axis=3, tiled=True)]
    all_gather x1 -> x0, blocking collectives: 20.2 us -> none  [per_device(): lax.all_gather(attended, ('attn', 'ffn'), axis=0, tiled=True)]
    unnamed x3 -> x0, waiting for transfers between devices: 18.7 us -> none
    psum x1 -> x0, blocking collectives: 17.7 us -> none  [per_device(): squares = lax.psum(jnp.sum(mixed * mixed, axis=1), 'attn')]
    broadcast_in_dim x67 -> x0, local copies, waits for them, and re-layouts: 4.46 us -> none  [the longest x32 2.24 us: per_device(): row_ends = jnp.repeat(ends, heads)]
  transfers between devices with their start and end apart: 2 -> 0, of which waited for: 2 -> 0; matrix products, arithmetic and copies ran while one was open for 0% -> 0% of each run, Pallas kernels for 0% -> 0%
where the time goes in v1:
time: 64.5 us; the launch traced here: 64.3 us
  Pallas kernels  62.4 us (97%)
  local copies, waits for them, and re-layouts  1.87 us (3%)
    pallas_call x1, Pallas kernels, per_device(): pl.pallas_call(functools.partial(kernel, n, tuple(sc)), out_shape=jax.Sha...  62.4 us
    unnamed x1, local copies, waits for them, and re-layouts  1.87 us

profile of v1, /device:TPU:0, one launch (start us, length us, event | category | flops | bytes accessed | tf_op | source)
XLA Modules:
  0.0 64.3 jit_solution(12753506334074956297)
XLA Ops:
  0.0 62.4 %shard_map.91 = f32[8,16384]{1,0:T(8,128)} custom-call(bf16[8,2048]{1,0:T(8,128)(2,1)} %refs_0_.1, bf16[2,8192,128]{2,1,0:T(8,128)(2,1)} %refs_1_.1, s32[8]{0:T(128)} %refs_2_.1, bf16[128,2048]{1,0:T(8,128)(2,1)} %refs_3_.1, bf16[2048,2048]{1,0:T(8,128)(2,1)} %refs_4_.1, bf16[2048]{0:T(1024)(128)(2,1)} %refs_5_.1, bf16[2048,1664]{1,0:T(8,128)(2,1)} %refs_6_.1, ...), custom_call_target="tpu_custom_call" | custom-call | tf_op jit(solution)/shard_map/pallas_call | solution.py:473
  62.4 1.9 %copy.11 = f32[8,16384]{1,0:T(8,128)} copy(f32[8,16384]{1,0:T(8,128)} %shard_map.91) | data formatting | bytes 1048576

commit v2 on v1

--- a/solution.py
+++ b/solution.py
@@ -17,7 +17,7 @@
 
 def unit_chunks(units):
     tiles = units // 128
-    marks = [0, (tiles * 3) // 13, (tiles * 7) // 13, (tiles * 11) // 13, tiles]
+    marks = [0, (tiles * 2) // 13, (tiles * 6) // 13, (tiles * 10) // 13, tiles]
     return [(lo * 128, (hi - lo) * 128) for lo, hi in zip(marks, marks[1:])]
 
 
@@ -115,6 +115,9 @@
     qr = req * heads
     cp_k.wait()
     cp_o.start()
+    cp_g.start()
+    cp_u.start()
+    cp_d.start()
 
     def first(k, m):
         off = pl.multiple_of(k * tc, tc)
@@ -131,9 +134,6 @@
     m = lax.fori_loop(0, slots // tc, first, jnp.full((qr, 128), NEG, F32))
     peak = jnp.max(m, axis=1, keepdims=True)
     cp_v.wait()
-    cp_g.start()
-    cp_u.start()
-    cp_d.start()
 
     scale2 = 1.4426950408889634 / math.sqrt(hd)
 

time: 64.5 us -> 65.9 us (1.022)
  Pallas kernels: 62.4 us -> 63.8 us
    pallas_call x1, Pallas kernels: 62.4 us -> 63.8 us  [per_device(): pl.pallas_call(functools.partial(kernel, n, tuple(sc)), out_shape=jax.Sha...]
where the time goes in v2:
time: 65.9 us; the launch traced here: 65.7 us
  Pallas kernels  63.8 us (97%)
  local copies, waits for them, and re-layouts  1.87 us (3%)
    pallas_call x1, Pallas kernels, per_device(): pl.pallas_call(functools.partial(kernel, n, tuple(sc)), out_shape=jax.Sha...  63.8 us
    unnamed x1, local copies, waits for them, and re-layouts  1.87 us

profile of v2, /device:TPU:0, one launch (start us, length us, event | category | flops | bytes accessed | tf_op | source)
XLA Modules:
  0.0 65.7 jit_solution(12267303982467723437)
XLA Ops:
  0.0 63.8 %shard_map.91 = f32[8,16384]{1,0:T(8,128)} custom-call(bf16[8,2048]{1,0:T(8,128)(2,1)} %refs_0_.1, bf16[2,8192,128]{2,1,0:T(8,128)(2,1)} %refs_1_.1, s32[8]{0:T(128)} %refs_2_.1, bf16[128,2048]{1,0:T(8,128)(2,1)} %refs_3_.1, bf16[2048,2048]{1,0:T(8,128)(2,1)} %refs_4_.1, bf16[2048]{0:T(1024)(128)(2,1)} %refs_5_.1, bf16[2048,1664]{1,0:T(8,128)(2,1)} %refs_6_.1, ...), custom_call_target="tpu_custom_call" | custom-call | tf_op jit(solution)/shard_map/pallas_call | solution.py:473
  63.8 1.9 %copy.11 = f32[8,16384]{1,0:T(8,128)} copy(f32[8,16384]{1,0:T(8,128)} %shard_map.91) | data formatting | bytes 1048576
